TPU v7x, 128 devices: a whole 4x4x4 slice. The times are simulated.
128 devices in a mesh: occ: 4 (over y_hi, core), aux: 32 (over x, z, y_lo).
Axes of the slice: x: 4, y: 4 (y_hi: 2, y_lo: 2; y = y_hi * 2 + y_lo), z: 4, core: 2. Of those that a mesh axis runs over, the one named last changes fastest.
Arguments:
- three_index: bfloat16 [12000, 6, 1920], P('aux'), may hold values from -0.47851562 to 0.47851562
- occ_energy: float32 [6], replicated, may hold values from -1.5 to -0.3
- vir_energy: float32 [1920], replicated, may hold values from 0.25 to 2.95
- batch_table: int32 [6], replicated, may hold values from 0 to 5, each once
- orbital_order: int32 [6], replicated, may hold values from 0 to 5, each once
- occ_pair_int: bfloat16 [2, 2, 12000], P(None, None, 'aux'), may hold values from -0.03881836 to 0.03881836
- half_ao: bfloat16 [2, 12000, 4000], P(None, 'aux'), may hold values from -9.536743e-06 to 9.536743e-06
- vir_coeff: bfloat16 [4000, 1920], P('aux', 'occ'), may hold values from -0.09375 to 0.09375
Outputs:
- gamma: bfloat16 [12000, 2, 1920], P('aux', None, 'occ')
- orbital_gradient: float32 [2, 1920], P(None, ('occ', 'aux'))
Inputs may be any that keep to these rules, and one draw needn't show every extreme that they name: `batch_table`: a permutation of 0 to 5; its first 4 entries are the partner orbitals of the window. `orbital_order`: a permutation of 0 to 5; its first 2 entries are the orbitals whose amplitudes are formed.
All inputs are finite; a program needn't handle non-finite values.
Results may differ from a plain program's by a relative error of at most 0.019.
Values may be sent and summed in bfloat16 or wider, within the bound.
No kernel may reach another device: no remote copies, remote signals or barrier semaphores. Data moves between devices by JAX's collectives and lax.ppermute only.
A program may use at most 128 MiB of HBM per device.

v0:
```python
import functools
import jax
import jax.numpy as jnp
from jax import lax
from jax.sharding import Mesh
from jax.sharding import PartitionSpec as P

NI = 2
NPART_DEV = 1
AUX = ("aux_0", "aux_1", "aux_2")
OCC = ("occ_0", "occ_1")
OCC_AUX = ("occ_0", "occ_1", "aux_0", "aux_1", "aux_2")


def own_rows(terms, axes):
    so_far = terms.astype(jnp.bfloat16)
    for axis in axes:
        so_far = lax.psum_scatter(so_far, axis, scatter_dimension=0, tiled=True)
    return so_far.astype(jnp.float32)


def one_axis_at_a_time(shard, axes):
    return functools.reduce(lax.psum, axes, shard)


def in_blocks(shard, dim, count):
    before, after = (shard.shape[:dim], shard.shape[dim + 1 :])
    return jnp.moveaxis(shard.reshape(*before, count, -1, *after), dim, 0)


def sent_and_summed(shard, axis, dim):
    count = lax.axis_size(axis)
    pieces = lax.all_to_all(in_blocks(shard, dim, count), axis, 0, 0, tiled=True)
    return jnp.sum(pieces, axis=0)


def local(
    three_index,
    occ_energy,
    vir_energy,
    batch_table,
    orbital_order,
    occ_pair_int,
    half_ao,
    vir_coeff,
):
    aux_width = lax.axis_size(AUX)
    nvirt = three_index.shape[2]
    row_share = nvirt // aux_width
    occ_place = lax.axis_index(OCC)
    aux_place = lax.axis_index(AUX)
    own_orbits = orbital_order[:NI]
    my_partners = lax.dynamic_slice_in_dim(batch_table, occ_place * NPART_DEV, NPART_DEV)
    left_block = jnp.take(three_index, own_orbits, axis=1)
    right_block = jnp.take(three_index, my_partners, axis=1)
    left_energy = jnp.take(occ_energy, own_orbits)
    right_energy = jnp.take(occ_energy, my_partners)
    pair_block = jnp.einsum(
        "qsa,qkb->askb", left_block, right_block, preferred_element_type=jnp.float32
    )
    pair_rows = own_rows(
        pair_block.reshape(row_share * lax.axis_size(AUX), NI * NPART_DEV * nvirt), AUX
    )
    row_count = pair_rows.shape[0]
    shaped = pair_rows.reshape(row_count, NI, NPART_DEV, nvirt)
    row_energy = lax.dynamic_slice_in_dim(vir_energy, aux_place * row_share, row_count)
    denominator = (
        row_energy[:, None, None, None]
        + vir_energy[None, None, None, :]
        - left_energy[None, :, None, None]
        - right_energy[None, None, :, None]
    )
    amps_rows = (-shaped / denominator).astype(jnp.bfloat16)
    gamma_part = jnp.einsum(
        "askb,qkb->qsa",
        lax.all_gather(amps_rows, AUX, axis=0, tiled=True),
        right_block,
        preferred_element_type=jnp.float32,
    )
    gamma_out = lax.psum_scatter(
        gamma_part.astype(jnp.bfloat16), OCC, scatter_dimension=2, tiled=True
    )
    density_part = -jnp.einsum(
        "askb,atkb->st", amps_rows, amps_rows, preferred_element_type=jnp.float32
    )
    density = one_axis_at_a_time(density_part, OCC_AUX)
    pair_int = occ_pair_int.astype(jnp.float32)
    coulomb = jnp.einsum("stq,st->q", pair_int, density, precision=lax.Precision.HIGHEST)
    exchange = jnp.einsum("suq,tu->stq", pair_int, density, precision=lax.Precision.HIGHEST)
    identity = jnp.eye(NI, dtype=jnp.float32)
    coefficient = (2.0 * identity[:, :, None] * coulomb[None, None, :] - exchange).astype(
        jnp.bfloat16
    )
    aux_rows = half_ao.shape[1]
    fock_part = jnp.dot(
        coefficient.reshape(NI, NI * aux_rows),
        half_ao.reshape(NI * aux_rows, half_ao.shape[2]),
        preferred_element_type=jnp.float32,
    )
    occ_side = -jnp.einsum(
        "usq,qua->sa", occ_pair_int, gamma_out, preferred_element_type=jnp.float32
    )
    fock_tile = sent_and_summed(fock_part, AUX, 1)
    vir_side = jnp.dot(fock_tile, vir_coeff.astype(jnp.float32), precision=lax.Precision.HIGHEST)
    gradient = sent_and_summed(occ_side + vir_side, AUX, 1)
    return (gamma_out, gradient)


def solution(mesh):
    torus = Mesh(mesh.devices.reshape(2, 2, 4, 4, 2), ("occ_0", "occ_1", "aux_0", "aux_1", "aux_2"))
    return jax.shard_map(
        local,
        mesh=torus,
        in_specs=(
            P(AUX, None, None),
            P(),
            P(),
            P(),
            P(),
            P(None, None, AUX),
            P(None, AUX, None),
            P(AUX, OCC),
        ),
        out_specs=(P(AUX, None, OCC), P(None, OCC_AUX)),
        check_vma=False,
    )
```

profile of v0, /device:TPU:0, one launch (start us, length us, event | category | flops | bytes accessed | tf_op | source)
XLA Modules:
  0.0 715.4 jit_solution(11130920844778028338)
XLA Ops:
  7.2 1.2 dynamic_slice.6
  10.4 0.7 compare_and_fusion
  11.1 4.5 gather_fusion
  15.6 12.4 %convolution_convert_fusion = bf16[1920,2,1920]{2,0,1:T(8,128)(2,1)} fusion(bf16[2,375,1920]{2,1,0:T(8,128)(2,1)S(1)} %gather_fusion, pred[2]{0:T(512)(128)(4,1)S(1)} %get-tuple-element.30, bf16[375,6,1920]{2,0,1:T(8,128)(2,1)} %param.8, s32[]{:T(128)} %bitcast.1, pred[]{:T(512)} %bitcast), kind=kOutput, calls=%fused_computation.5 | convolution fusion | flops 5539132928 | bytes 19070466 | tf_op jit(solution)/shard_map/qsa,qkb->askb/dot_general | solution.py:58
  27.9 20.1 %copy.19 = bf16[1920,3840]{1,0:T(8,128)(2,1)} copy(bf16[1920,3840]{0,1:T(8,128)(2,1)} %bitcast.75) | data formatting | bytes 29491200 | tf_op jit(solution)/shard_map/convert_element_type | solution.py:16
  48.2 134.6 %reduce-scatter.5.cloned.1.call-done = bf16[480,3840]{1,0:T(8,128)(2,1)} async-done(((bf16[1920,3840]{1,0:T(8,128)(2,1)}), bf16[480,3840]{1,0:T(8,128)(2,1)}) %reduce-scatter.5.cloned.1.call-update) | async-done | bytes 3686416 | tf_op jit(solution)/shard_map/reduce_scatter | solution.py:18
  182.8 0.6 gather_fusion.1
  183.5 0.1 dynamic_slice.7
  183.5 0.1 broadcast_add_fusion
  183.6 44.2 %reduce-scatter.7.cloned.1.call-done = bf16[120,3840]{1,0:T(8,128)(2,1)} async-done(((bf16[480,3840]{1,0:T(8,128)(2,1)}), bf16[120,3840]{1,0:T(8,128)(2,1)}) %reduce-scatter.7.cloned.1.call-update) | async-done | bytes 921616 | tf_op jit(solution)/shard_map/reduce_scatter | solution.py:18
  227.9 16.9 %fusion = bf16[64,3840]{1,0:T(8,128)(2,1)S(1)} fusion(bf16[120,3840]{1,0:T(8,128)(2,1)} %reduce-scatter.7.cloned.1.call-done), kind=kCustom, calls=%all-reduce-scatter | all-reduce-scatter fusion | flops 491521 | bytes 1413632
  244.8 2.4 collective-permute-start
  247.2 0.6 dynamic-slice.6
  247.8 0.3 sub.72
  248.1 0.3 pad.7
  248.6 0.7 dynamic-slice.13
  250.7 0.7 concatenate.2
  251.4 1.1 divide_convert_fusion
  252.5 0.5 neg.28
  253.0 1.5 fusion.29
  254.5 0.2 all-reduce.5.cloned.1.call-start
  254.7 317.7 %all-gather.2.cloned.1.call-done = bf16[1920,2,1,1920]{3,1,2,0:T(2,128)(2,1)} async-done(((bf16[60,2,1,1920]{3,1,2,0:T(2,128)(2,1)}), bf16[1920,2,1,1920]{3,1,2,0:T(2,128)(2,1)}) %all-gather.2.cloned.1.call-update) | async-done | bytes 14745616 | tf_op jit(solution)/shard_map/all_gather | solution.py:76
  572.4 13.1 %fusion.9 = bf16[375,2,1920]{2,0,1:T(8,128)(2,1)S(1)} fusion(bf16[1920,2,1,1920]{3,1,2,0:T(2,128)(2,1)} %all-gather.2.cloned.1.call-done, bf16[375,6,1920]{2,0,1:T(8,128)(2,1)} %param.8, s32[]{:T(128)} %bitcast.1, pred[]{:T(512)} %bitcast), kind=kOutput, calls=%fused_computation.9 | convolution fusion | flops 5531759616 | bytes 19070464 | tf_op jit(solution)/shard_map/askb,qkb->qsa/dot_general | solution.py:74
  585.6 7.0 copy.22
  592.6 0.2 convert_element_type.56
  592.8 1.6 fusion.25
  594.3 6.4 psum.35
  600.8 2.4 psum.36
  603.2 10.0 %copy.24 = bf16[2,375,4000]{2,1,0:T(8,128)(2,1)} copy(bf16[2,375,4000]{2,0,1:T(2,128)(2,1)} %param.14) | data formatting | bytes 12000000 | tf_op args[6]
  613.2 10.7 %psum.37 = f32[2,2]{1,0:T(2,128)S(1)} all-reduce(f32[2,2]{1,0:T(2,128)S(1)} %psum.36), channel_id=1, replica_groups=mesh['occ_0'=2,'occ_1'=2,'aux_0'=4,'aux_1'=4,'aux_2'=2] {'aux_0'}, use_global_device_ids=true, to_apply=%region_6.7 | all-reduce | flops 4 | bytes 32 | tf_op jit(solution)/shard_map/psum | solution.py:23
  623.9 8.1 %reshape.144 = bf16[750,4000]{1,0:T(8,128)(2,1)} reshape(bf16[2,375,4000]{2,1,0:T(8,128)(2,1)} %copy.24) | data formatting | bytes 12000000 | tf_op jit(solution)/shard_map/reshape | solution.py:97
  632.0 10.6 %psum.38 = f32[2,2]{1,0:T(2,128)S(1)} all-reduce(f32[2,2]{1,0:T(2,128)S(1)} %psum.37), channel_id=1, replica_groups=mesh['occ_0'=2,'occ_1'=2,'aux_0'=4,'aux_1'=4,'aux_2'=2] {'aux_1'}, use_global_device_ids=true, to_apply=%region_7.8 | all-reduce | flops 4 | bytes 32 | tf_op jit(solution)/shard_map/psum | solution.py:23
  642.7 28.6 %dot_general.35 = bf16[32,125,750]{1,0,2:T(8,128)(2,1)} reshape(bf16[4000,750]{0,1:T(8,128)(2,1)} %bitcast.74) | data formatting | bytes 12000000 | tf_op jit(solution)/shard_map/dot_general | solution.py:95
  671.3 5.0 psum.39
  676.3 0.2 convolution_reduce_fusion
  676.5 0.1 fusion.22
  676.7 0.1 reshape.228
  676.8 5.1 fusion.18
  681.8 3.9 all-to-all-start
  685.7 0.6 dynamic-slice.9
  686.9 7.0 all-to-all-done
  694.0 1.6 constant_dynamic-slice_fusion
  695.6 0.1 copy.27
  695.8 0.3 fusion.24
  696.0 0.3 convolution_add_fusion
  696.3 0.2 reshape.145
  696.5 11.7 %all_to_all.10 = f32[32,2,15]{2,1,0:T(2,128)S(1)} all-to-all(f32[32,2,15]{2,1,0:T(2,128)S(1)} %copy.26), channel_id=1, replica_groups=mesh['occ_0'=2,'occ_1'=2,'aux_0'=4,'aux_1'=4,'aux_2'=2] {'aux_0','aux_1'..., dimensions={0} | all-to-all | bytes 7680 | tf_op jit(solution)/shard_map/all_to_all | solution.py:33
  708.2 0.6 reduce_sum.19
  (34 shorter events, 0.5 us)
Async XLA Ops:
  7.2 688.9 %copy-start = (bf16[125,480]{0,1:T(8,128)(2,1)S(1)}, bf16[125,480]{0,1:T(8,128)(2,1)}, u32[]{:S(2)}) copy-start(bf16[125,480]{0,1:T(8,128)(2,1)} %param.15) | copy-start | bytes 360004
  7.2 175.5 %reduce-scatter.5.cloned.1.call-start = ((), (), s32[]{:S(2)}) async-start(), calls=%async_computation.4 | async-start | bytes 18432000 | tf_op jit(solution)/shard_map/reduce_scatter | solution.py:18
  48.1 134.7 %copy-start.1 = (f32[6]{0:T(128)S(1)}, f32[6]{0:T(128)}, u32[]{:S(2)}) copy-start(f32[6]{0:T(128)} %param.9) | copy-start | bytes 76
  48.1 135.4 %copy-start.4 = (f32[1920]{0:T(1024)S(1)}, f32[1920]{0:T(1024)}, u32[]{:S(2)}) copy-start(f32[1920]{0:T(1024)} %param.10) | copy-start | bytes 23044
  48.1 179.8 %reduce-scatter.7.cloned.1.call-start = ((), (), s32[]{:S(2)}) async-start(), calls=%async_computation.5 | async-start | bytes 4608000 | tf_op jit(solution)/shard_map/reduce_scatter | solution.py:18
  182.7 65.9 %copy-start.6 = (u32[128]{0:T(128)S(1)}, u32[128]{0:T(128)}, u32[]{:S(2)}) copy-start(u32[128]{0:T(128)} %constant.137) | copy-start | bytes 1540
  182.7 389.7 %all-gather.2.cloned.1.call-start = ((), (), s32[]{:S(2)}) async-start(), calls=%async_computation.6 | async-start | bytes 15206400 | tf_op jit(solution)/shard_map/all_gather | solution.py:76
  244.8 5.9 collective-permute-start
  254.5 439.5 %all-reduce.5.cloned.1.call-start = ((), (), s32[]{:S(2)}) async-start(), calls=%async_computation.7 | async-start | bytes 5898240
  585.6 7.0 copy-start.3
  642.7 33.6 %copy-start.5 = (bf16[2,2,375]{2,1,0:T(2,128)(2,1)S(1)}, bf16[2,2,375]{2,1,0:T(2,128)(2,1)}, u32[]{:S(2)}) copy-start(bf16[2,2,375]{2,1,0:T(2,128)(2,1)} %param.13) | copy-start | bytes 9004
  671.3 14.4 %copy-start.7 = (u32[128]{0:T(128)S(1)}, u32[128]{0:T(128)}, u32[]{:S(2)}) copy-start(u32[128]{0:T(128)} %constant.141) | copy-start | bytes 1540
  681.8 12.1 %all-to-all-start = ((f32[32,2,125]{2,1,0:T(2,128)}), f32[32,2,125]{2,1,0:T(2,128)S(1)}, u32[]{:S(2)}, u32[]{:S(2)}) async-start(f32[32,2,125]{2,1,0:T(2,128)} %fusion.18), calls=%async_computation.2 | async-start | bytes 65536 | tf_op jit(solution)/shard_map/all_to_all | solution.py:33
  695.7 13.1 %copy-start.2 = (bf16[375,2,480]{0,2,1:T(8,128)(2,1)}, bf16[375,2,480]{0,2,1:T(8,128)(2,1)S(1)}, u32[]{:S(2)}) copy-start(bf16[375,2,480]{0,2,1:T(8,128)(2,1)S(1)} %copy.27) | copy-start | bytes 2160004
Sparse Core Ops, SparseCore 0:
  48.2 134.4 reduce-scatter.4
  185.1 42.6 reduce-scatter.6
  254.6 317.7 all-gather.1
  592.7 75.0 all-reduce.4
where the time goes:
time: 717 us; the launch traced here: 715 us
  waiting for transfers between devices  504 us (70%)
  local copies, waits for them, and re-layouts  86.4 us (12%)
  blocking collectives  63.8 us (9%)
  matrix products  33 us (5%)
  between operations  18 us (3%)
    all_gather x1, waiting for transfers between devices, local(): lax.all_gather(amps_rows, AUX, axis=0, tiled=True)  318 us
    reduce_scatter x2, waiting for transfers between devices, own_rows(): so_far = lax.psum_scatter(so_far, axis, scatter_dimension=0, tiled=True)  179 us
    psum x5, blocking collectives, one_axis_at_a_time(): return functools.reduce(lax.psum, axes, shard)  35.2 us
    dot_general x1, local copies, waits for them, and re-layouts, local(): jnp.dot(coefficient.reshape(NI, NI * aux_rows), half_ao.reshape(NI * aux_...  28.6 us
    convert_element_type x1, local copies, waits for them, and re-layouts, own_rows(): so_far = terms.astype(jnp.bfloat16)  20.1 us
    unnamed x1, blocking collectives  16.9 us
  transfers between devices with their start and end apart: 6, of which 4 were waited for; matrix products, arithmetic and copies ran while one was open for 8% of the time, Pallas kernels for 0%

commit v1 on v0

--- a/solution.py
+++ b/solution.py
@@ -73,7 +73,9 @@
     amps_rows = (-shaped / denominator).astype(jnp.bfloat16)
     gamma_part = jnp.einsum(
         "askb,qkb->qsa",
-        lax.all_gather(amps_rows, AUX, axis=0, tiled=True),
+        jnp.concatenate(
+            lax.all_to_all(jnp.stack([amps_rows] * lax.axis_size(AUX)), AUX, 0, 0), axis=0
+        ),
         right_block,
         preferred_element_type=jnp.float32,
     )

time: 717 us -> 600 us (0.84)
  waiting for transfers between devices: 504 us -> 228 us
  blocking collectives: 63.8 us -> 217 us
  local copies, waits for them, and re-layouts: 86.4 us -> 98 us
    all_gather x1 -> x0, waiting for transfers between devices: 318 us -> none  [local(): lax.all_gather(amps_rows, AUX, axis=0, tiled=True)]
    unnamed x6 -> x8, waiting for transfers between devices: 0.08 us -> 221 us
    reduce_scatter x2 -> x0, waiting for transfers between devices: 179 us -> none  [own_rows(): so_far = lax.psum_scatter(so_far, axis, scatter_dimension=0, tiled=True)]
    all_to_all x0 -> x1, blocking collectives: none -> 172 us  [local(): lax.all_to_all(jnp.stack([amps_rows] * lax.axis_size(AUX)), AUX, 0, 0)]
    unnamed x25 -> x21, local copies, waits for them, and re-layouts: 14.2 us -> 35.1 us
    convert_element_type x1 -> x0, local copies, waits for them, and re-layouts: 20.1 us -> none  [own_rows(): so_far = terms.astype(jnp.bfloat16)]
    unnamed x1 -> x0, blocking collectives: 16.9 us -> none
    another operation x0 -> x1, local copies, waits for them, and re-layouts: none -> 8.15 us  [local(): jnp.stack([amps_rows] * lax.axis_size(AUX))]
  transfers between devices with their start and end apart: 6 -> 5, of which waited for: 4 -> 4; matrix products, arithmetic and copies ran while one was open for 8% -> 10% of each run, Pallas kernels for 0% -> 0%
where the time goes in v1:
time: 600 us; the launch traced here: 599 us
  waiting for transfers between devices  228 us (38%)
  blocking collectives  217 us (36%)
  local copies, waits for them, and re-layouts  98 us (16%)
  matrix products  29.5 us (5%)
  between operations  17.8 us (3%)
    unnamed x8, waiting for transfers between devices  221 us
    all_to_all x1, blocking collectives, local(): lax.all_to_all(jnp.stack([amps_rows] * lax.axis_size(AUX)), AUX, 0, 0)  172 us
    unnamed x21, local copies, waits for them, and re-layouts  35.1 us
    psum x5, blocking collectives, one_axis_at_a_time(): return functools.reduce(lax.psum, axes, shard)  33.3 us
    dot_general x1, local copies, waits for them, and re-layouts, local(): jnp.dot(coefficient.reshape(NI, NI * aux_rows), half_ao.reshape(NI * aux_...  28.5 us
    dot_general x1, matrix products, local(): jnp.einsum('qsa,qkb->askb', left_block, right_block, preferred_element_ty...  12.4 us
  transfers between devices with their start and end apart: 5, of which 4 were waited for; matrix products, arithmetic and copies ran while one was open for 10% of the time, Pallas kernels for 0%

profile of v1, /device:TPU:0, one launch (start us, length us, event | category | flops | bytes accessed | tf_op | source)
XLA Modules:
  0.0 598.6 jit_solution(8467800016916589284)
XLA Ops:
  7.2 1.2 dynamic_slice.6
  10.4 0.7 compare_and_fusion
  11.1 4.5 gather_fusion
  15.6 12.4 %convolution_convert_fusion = bf16[1920,2,1920]{2,0,1:T(8,128)(2,1)} fusion(bf16[2,375,1920]{2,1,0:T(8,128)(2,1)S(1)} %gather_fusion, pred[2]{0:T(512)(128)(4,1)S(1)} %get-tuple-element.30, bf16[375,6,1920]{2,0,1:T(8,128)(2,1)} %param.8, s32[]{:T(128)} %bitcast.1, pred[]{:T(512)} %bitcast), kind=kOutput, calls=%fused_computation.4 | convolution fusion | flops 5539132928 | bytes 19070466 | tf_op jit(solution)/shard_map/qsa,qkb->askb/dot_general | solution.py:58
  27.9 20.1 %copy.32 = bf16[1920,3840]{1,0:T(8,128)(2,1)} copy(bf16[1920,3840]{0,1:T(8,128)(2,1)} %bitcast.77) | data formatting | bytes 29491200
  48.1 0.0 reduce-scatter.10.cloned.1.call-start
  48.2 134.6 %reduce-scatter.8.cloned.1.call-done = bf16[480,3840]{1,0:T(8,128)(2,1)} async-done(((bf16[1920,3840]{1,0:T(8,128)(2,1)}), bf16[480,3840]{1,0:T(8,128)(2,1)}) %reduce-scatter.8.cloned.1.call-update) | async-done | bytes 3686416
  182.8 45.1 %reduce-scatter.10.cloned.1.call-done = bf16[120,3840]{1,0:T(8,128)(2,1)} async-done(((bf16[480,3840]{1,0:T(8,128)(2,1)}), bf16[120,3840]{1,0:T(8,128)(2,1)}) %reduce-scatter.10.cloned.1.call-update) | async-done | bytes 921616
  227.9 2.2 copy.35
  230.1 0.0 all-reduce.7.cloned.1.call-start
  230.2 0.6 dynamic-slice.6
  230.8 0.6 gather_fusion.1
  231.4 0.1 sub.69
  232.2 0.1 dynamic_slice.7
  232.3 0.6 dynamic-slice.7
  233.6 0.3 broadcast_add_fusion
  233.9 41.3 %all-reduce.5.cloned.1.call-done = bf16[120,3840]{0,1:T(8,128)(2,1)} async-done(((bf16[120,3840]{0,1:T(8,128)(2,1)}), bf16[120,3840]{0,1:T(8,128)(2,1)}) %all-reduce.5.cloned.1.call-update) | async-done | bytes 921616
  275.2 2.0 fusion.15
  277.2 0.4 divide_convert_fusion
  277.6 1.0 copy.21
  278.6 8.2 %stack.2 = bf16[32,60,2,1,1920]{4,2,1,3,0:T(2,128)(2,1)S(1)} broadcast(bf16[60,2,1920]{2,1,0:T(2,128)(2,1)S(1)} %copy.21), dimensions={1,2,4} | broadcast | bytes 15206400 | tf_op jit(solution)/shard_map/stack | solution.py:77
  286.8 172.1 %all_to_all.15 = bf16[32,60,2,1,1920]{4,2,1,3,0:T(2,128)(2,1)S(1)} all-to-all(bf16[32,60,2,1,1920]{4,2,1,3,0:T(2,128)(2,1)S(1)} %stack.2), channel_id=1, replica_groups=mesh['occ_0'=2,'occ_1'=2,'aux_0'=4,'aux_1'=4,'aux_2'=2] {'aux_0','aux_1'..., dimensions={0} | all-to-all | bytes 29491200 | tf_op jit(solution)/shard_map/all_to_all | solution.py:77
  458.9 9.6 %fusion.7 = bf16[375,2,1920]{2,0,1:T(8,128)(2,1)} fusion(bf16[1920,2,1920]{2,1,0:T(2,128)(2,1)S(1)} %bitcast.76, bf16[375,6,1920]{2,0,1:T(8,128)(2,1)} %param.8, s32[]{:T(128)} %bitcast.1, pred[]{:T(512)} %bitcast), kind=kOutput, calls=%fused_computation.8 | convolution fusion | flops 5531759616 | bytes 19070464 | tf_op jit(solution)/shard_map/askb,qkb->qsa/dot_general | solution.py:74
  468.5 8.7 %copy.23 = bf16[375,2,1920]{0,1,2:T(2,128)(2,1)} copy(bf16[375,2,1920]{2,0,1:T(8,128)(2,1)} %fusion.7) | data formatting | bytes 5760000 | tf_op jit(solution)/shard_map/convert_element_type | solution.py:83
  477.2 1.0 copy.25
  478.2 1.6 fusion.26
  479.8 6.4 %psum.35 = f32[2,2]{1,0:T(2,128)S(1)} all-reduce(f32[2,2]{1,0:T(2,128)S(1)} %fusion.26), channel_id=1, replica_groups=mesh['occ_0'=2,'occ_1'=2,'aux_0'=4,'aux_1'=4,'aux_2'=2] {'occ_0'}, use_global_device_ids=true, to_apply=%region_4.5 | all-reduce | flops 4 | bytes 32 | tf_op jit(solution)/shard_map/psum | solution.py:23
  486.2 2.4 psum.36
  488.7 9.7 %copy.27 = bf16[2,375,4000]{2,1,0:T(8,128)(2,1)} copy(bf16[2,375,4000]{2,0,1:T(2,128)(2,1)} %param.14) | data formatting | bytes 12000000 | tf_op args[6]
  498.4 11.4 %psum.37 = f32[2,2]{1,0:T(2,128)S(1)} all-reduce(f32[2,2]{1,0:T(2,128)S(1)} %psum.36), channel_id=1, replica_groups=mesh['occ_0'=2,'occ_1'=2,'aux_0'=4,'aux_1'=4,'aux_2'=2] {'aux_0'}, use_global_device_ids=true, to_apply=%region_6.7 | all-reduce | flops 4 | bytes 32 | tf_op jit(solution)/shard_map/psum | solution.py:23
  509.7 8.1 %reshape.137 = bf16[750,4000]{1,0:T(8,128)(2,1)} reshape(bf16[2,375,4000]{2,1,0:T(8,128)(2,1)} %copy.27) | data formatting | bytes 12000000 | tf_op jit(solution)/shard_map/reshape | solution.py:99
  517.9 8.2 %psum.38 = f32[2,2]{1,0:T(2,128)S(1)} all-reduce(f32[2,2]{1,0:T(2,128)S(1)} %psum.37), channel_id=1, replica_groups=mesh['occ_0'=2,'occ_1'=2,'aux_0'=4,'aux_1'=4,'aux_2'=2] {'aux_1'}, use_global_device_ids=true, to_apply=%region_7.8 | all-reduce | flops 4 | bytes 32 | tf_op jit(solution)/shard_map/psum | solution.py:23
  526.1 28.5 %dot_general.35 = bf16[32,125,750]{1,0,2:T(8,128)(2,1)} reshape(bf16[4000,750]{0,1:T(8,128)(2,1)} %bitcast.75) | data formatting | bytes 12000000 | tf_op jit(solution)/shard_map/dot_general | solution.py:97
  554.6 4.9 psum.39
  559.5 0.2 convolution_reduce_fusion
  559.7 0.1 fusion.23
  559.9 0.1 reshape.221
  560.0 5.1 fusion.19
  565.0 3.9 all-to-all-start.1
  568.9 0.6 dynamic-slice.9
  570.2 7.0 %all-to-all-done.1 = f32[32,2,125]{2,1,0:T(2,128)S(1)} async-done(((f32[32,2,125]{2,1,0:T(2,128)}), f32[32,2,125]{2,1,0:T(2,128)S(1)}, u32[]{:S(2)}, u32[]{:S(2)}) %all-to-all-start.1) | async-done | bytes 32032 | tf_op jit(solution)/shard_map/all_to_all | solution.py:33
  577.2 1.6 constant_dynamic-slice_fusion
  578.9 0.1 copy.30
  579.0 0.3 fusion.25
  579.3 0.3 convolution_add_fusion
  579.5 0.2 reshape.138
  579.7 11.7 %all_to_all.16 = f32[32,2,15]{2,1,0:T(2,128)S(1)} all-to-all(f32[32,2,15]{2,1,0:T(2,128)S(1)} %copy.29), channel_id=1, replica_groups=mesh['occ_0'=2,'occ_1'=2,'aux_0'=4,'aux_1'=4,'aux_2'=2] {'aux_0','aux_1'..., dimensions={0} | all-to-all | bytes 7680 | tf_op jit(solution)/shard_map/all_to_all | solution.py:33
  591.4 0.6 reduce_sum.19
  (27 shorter events, 0.3 us)
Async XLA Ops:
  7.2 572.1 %copy-start = (bf16[125,480]{0,1:T(8,128)(2,1)S(1)}, bf16[125,480]{0,1:T(8,128)(2,1)}, u32[]{:S(2)}) copy-start(bf16[125,480]{0,1:T(8,128)(2,1)} %param.15) | copy-start | bytes 360004
  7.2 175.5 %reduce-scatter.8.cloned.1.call-start = ((), (), s32[]{:S(2)}) async-start(), calls=%async_computation.5 | async-start | bytes 18432000
  48.1 179.8 %reduce-scatter.10.cloned.1.call-start = ((), (), s32[]{:S(2)}) async-start(), calls=%async_computation.6 | async-start | bytes 4608000
  182.7 47.5 %copy-start.1 = (f32[6]{0:T(128)S(1)}, f32[6]{0:T(128)}, u32[]{:S(2)}) copy-start(f32[6]{0:T(128)} %param.9) | copy-start | bytes 76
  182.7 49.5 %copy-start.3 = (f32[1920]{0:T(1024)S(1)}, f32[1920]{0:T(1024)}, u32[]{:S(2)}) copy-start(f32[1920]{0:T(1024)} %param.10) | copy-start | bytes 23044
  182.7 49.6 %copy-start.6 = (u32[128]{0:T(128)S(1)}, u32[128]{0:T(128)}, u32[]{:S(2)}) copy-start(u32[128]{0:T(128)} %constant.137) | copy-start | bytes 1540
  182.7 92.4 %all-reduce.5.cloned.1.call-start = ((), (), s32[]{:S(2)}) async-start(), calls=%async_computation.7 | async-start | bytes 1966080
  230.1 347.1 %all-reduce.7.cloned.1.call-start = ((), (), s32[]{:S(2)}) async-start(), calls=%async_computation.8 | async-start | bytes 5898240
  526.1 33.4 %copy-start.4 = (bf16[2,2,375]{2,1,0:T(2,128)(2,1)S(1)}, bf16[2,2,375]{2,1,0:T(2,128)(2,1)}, u32[]{:S(2)}) copy-start(bf16[2,2,375]{2,1,0:T(2,128)(2,1)} %param.13) | copy-start | bytes 9004
  560.0 9.0 %copy-start.5 = (u32[128]{0:T(128)S(1)}, u32[128]{0:T(128)}, u32[]{:S(2)}) copy-start(u32[128]{0:T(128)} %constant.141) | copy-start | bytes 1540
  565.0 12.1 %all-to-all-start.1 = ((f32[32,2,125]{2,1,0:T(2,128)}), f32[32,2,125]{2,1,0:T(2,128)S(1)}, u32[]{:S(2)}, u32[]{:S(2)}) async-start(f32[32,2,125]{2,1,0:T(2,128)} %fusion.19), calls=%async_computation.1 | async-start | bytes 65536 | tf_op jit(solution)/shard_map/all_to_all | solution.py:33
  579.0 13.1 %copy-start.2 = (bf16[375,2,480]{0,2,1:T(8,128)(2,1)}, bf16[375,2,480]{0,2,1:T(8,128)(2,1)S(1)}, u32[]{:S(2)}) copy-start(bf16[375,2,480]{0,2,1:T(8,128)(2,1)S(1)} %copy.30) | copy-start | bytes 2160004
Sparse Core Ops, SparseCore 0:
  48.2 134.4 reduce-scatter.7
  185.1 42.6 reduce-scatter.9
  230.3 44.7 all-reduce.4
  477.4 71.7 all-reduce.6
